TPU v7x, 32 devices: a whole 2x2x4 slice. The times are simulated.
32 devices in a mesh: ind: 16 (over z, y, x), snp: 2 (over core).
Axes of the slice: x: 2, y: 2, z: 4, core: 2. Of those that a mesh axis runs over, the one named last changes fastest.
Arguments:
- genotypes: int32 [1024, 4096], P('ind', 'snp'), may hold values from 0 to 2
- observed: int32 [1024, 4096], P('ind', 'snp'), may hold values from 0 to 1
- ancestry: float32 [1024, 32], P('ind'), may hold values from 0.018 to 54.6, as said below
- freqs: float32 [4096, 32], P(('snp', 'ind')), may hold values from 0.05 to 0.95
Outputs:
- ancestry_out: float32 [1024, 32], P('ind')
- freqs_out: float32 [4096, 32], P(('snp', 'ind'))
Inputs may be any that keep to these rules, and one draw needn't show every extreme that they name: `ancestry`: positive weights.
All inputs are finite; a program needn't handle non-finite values.
Results may differ from a plain program's by a relative error of at most 0.0003.
Values sent between devices are 32-bit elements; how exact they have to be, the bound alone decides.
A program may use at most 64 MiB of HBM per device.

v0:
```python
import functools

import jax
import jax.numpy as jnp
from jax import lax
from jax.experimental import pallas as pl
from jax.experimental.pallas import tpu as pltpu
from jax.sharding import PartitionSpec as P

STEPS = 3


clip_low = 1e-05
high = lax.Precision.HIGHEST
MESH = pl.DeviceIdType.MESH
f32 = jnp.float32
bf16 = jnp.bfloat16


def over_rows(left, right):
    return lax.dot_general(
        left, right, (((0,), (0,)), ((), ())), precision=high, preferred_element_type=jnp.float32
    )


def per_device(genotypes, observed, ancestry, freqs):
    ind_count = lax.axis_size("ind")
    snp_count = lax.axis_size("snp")
    geno = genotypes.astype(jnp.float32)
    seen = observed.astype(jnp.float32)
    hits = seen * geno
    misses = seen * (2.0 - geno)
    own_rows = freqs.shape[0]
    q_zero = ancestry / jnp.sum(ancestry, axis=1, keepdims=True)
    f_zero = lax.all_gather(freqs, "ind", axis=0, tiled=True)
    f_weight = 1.0 / ind_count
    q_weight = 1.0 / snp_count

    def em_map(q_rows, f_state):
        prob = jnp.dot(q_rows, f_state.T, precision=high, preferred_element_type=jnp.float32)
        ratio_a = hits / prob
        ratio_b = misses / (1.0 - prob)
        sum_a = jnp.dot(ratio_a, f_state, precision=high, preferred_element_type=jnp.float32)
        sum_b = jnp.dot(ratio_b, 1.0 - f_state, precision=high, preferred_element_type=jnp.float32)
        c_part = over_rows(ratio_a, q_rows)
        d_part = over_rows(ratio_b, q_rows)
        sum_a, sum_b = lax.psum((sum_a, sum_b), "snp")
        q_next = q_rows * (sum_a + sum_b)
        q_next = q_next / jnp.sum(q_next, axis=1, keepdims=True)
        c_total, d_total = lax.psum((c_part, d_part), "ind")
        f_next = f_state * c_total / (f_state * c_total + (1.0 - f_state) * d_total)
        return (q_next, f_next)

    for step in range(STEPS):
        q_one, f_one = em_map(q_zero, f_zero)
        rq = q_one - q_zero
        rf = f_one - f_zero
        first_local = q_weight * jnp.sum(rq * rq) + f_weight * jnp.sum(rf * rf)
        q_two, f_two = em_map(q_one, f_one)
        vq = q_two - 2.0 * q_one + q_zero
        vf = f_two - 2.0 * f_one + f_zero
        second_local = q_weight * jnp.sum(vq * vq) + f_weight * jnp.sum(vf * vf)
        first, second = lax.psum((first_local, second_local), ("ind", "snp"))
        alpha = -jnp.sqrt(first / (second + 1e-20))
        q_ext = jnp.clip(q_zero - 2.0 * alpha * rq + alpha * alpha * vq, clip_low, 1.0 - clip_low)
        q_zero = q_ext / jnp.sum(q_ext, axis=1, keepdims=True)
        f_zero = jnp.clip(f_zero - 2.0 * alpha * rf + alpha * alpha * vf, clip_low, 1.0 - clip_low)
    f_final = lax.dynamic_slice_in_dim(f_zero, lax.axis_index("ind") * own_rows, own_rows, 0)
    return (q_zero, f_final)


def split3(x):
    one = x.astype(bf16)
    rest = x - one.astype(f32)
    two = rest.astype(bf16)
    three = (rest - two.astype(f32)).astype(bf16)
    return one, two, three


def nn(left, right):
    return jnp.dot(left, right, preferred_element_type=f32)


def nt(left, right):
    return lax.dot_general(left, right, (((1,), (1,)), ((), ())), preferred_element_type=f32)


def total_of(x):
    return jnp.sum(jnp.sum(x, axis=1, keepdims=True), axis=0, keepdims=True)


def kernel(
    inds, geno_ref, obs_ref, anc_ref, freq_ref, q_out, f_out,
    geno_all, obs_all, anc_all, hits, misses, part, pair_in, mine, scat_in, full,
    q_zero, q_one, f_zero, f_one, flip,
    anc_send, geno_send, obs_send, geno_recv, obs_recv, anc_recv,
    pair_send, pair_recv, scat_send, scat_recv, gath_send, gath_recv, fwd_send, fwd_recv,
):
    me = lax.axis_index("ind")
    core = lax.axis_index("snp")
    other = 1 - core
    rows = geno_ref.shape[0]
    blocks = hits.shape[0]
    kdim = anc_ref.shape[1]
    peers = [lax.rem(me + d, inds) for d in range(1, inds)]

    barrier = pltpu.get_barrier_semaphore()
    for j in peers:
        pl.semaphore_signal(barrier, inc=1, device_id=(j, core), device_id_type=MESH)
    pl.semaphore_signal(barrier, inc=1, device_id=(me, other), device_id_type=MESH)
    pl.semaphore_wait(barrier, inds)

    def send(src, dst, ssem, rsem, dev):
        copy = pltpu.make_async_remote_copy(
            src_ref=src, dst_ref=dst, send_sem=ssem, recv_sem=rsem,
            device_id=dev, device_id_type=MESH,
        )
        copy.start()
        return copy

    def arrived(ref, sem):
        pltpu.make_async_copy(ref, ref, sem).wait()

    most = pl.ds(0, inds - 1)
    for j in peers:
        send(anc_ref, anc_all.at[me], anc_send, anc_recv, (j, core))
    for j in peers:
        cols = pl.ds(pl.multiple_of(j * 128, 128), 128)
        send(geno_ref.at[:, cols], geno_all.at[me], geno_send, geno_recv, (j, core))
        send(obs_ref.at[:, cols], obs_all.at[me], obs_send, obs_recv, (j, core))
    own = pl.ds(pl.multiple_of(me * 128, 128), 128)
    geno_all[me] = geno_ref[:, own]
    obs_all[me] = obs_ref[:, own]
    anc_all[me] = anc_ref[...]
    f_zero[...] = freq_ref[...]
    arrived(anc_all.at[most], anc_recv)
    arrived(geno_all.at[most], geno_recv)
    arrived(obs_all.at[most], obs_recv)
    for block in range(blocks):
        anc = jnp.concatenate([anc_all[2 * block], anc_all[2 * block + 1]], axis=0).T
        q_zero[:, 128 * block : 128 * block + 128] = anc / jnp.sum(anc, axis=0, keepdims=True)
        geno = jnp.concatenate([geno_all[2 * block], geno_all[2 * block + 1]], axis=0).astype(f32).T
        seen = jnp.concatenate([obs_all[2 * block], obs_all[2 * block + 1]], axis=0).astype(f32).T
        hits[block] = seen * geno
        misses[block] = seen * (2.0 - geno)
    arrived(anc_all.at[most], anc_send)
    arrived(geno_all.at[most], geno_send)
    arrived(obs_all.at[most], obs_send)

    lane = lax.broadcasted_iota(jnp.int32, (1, 128), 1)

    def em_map(e, q_ref, f, extra_of):
        ft = f.T
        f1, f2, f3 = split3(ft)
        lhs = jnp.concatenate([x.astype(f32) for x in (f1, f2, f1, f2, f3, f1, f3, f2)], axis=0).T.astype(bf16)
        g1, g2, g3 = split3(jnp.concatenate([ft, 1.0 - ft], axis=1))
        g64 = jnp.concatenate([g1, g2], axis=0)
        g96 = jnp.concatenate([g1, g2, g3], axis=0)
        cd = jnp.zeros((256, kdim), f32)
        for chunk in range(blocks // 2):
            q1, q2, q3 = split3(q_ref[:, 256 * chunk : 256 * chunk + 256])
            prob = nn(lhs, jnp.concatenate([q1, q1, q2, q2, q1, q3, q2, q3], axis=0))
            hit = jnp.concatenate([hits[2 * chunk], hits[2 * chunk + 1]], axis=1)
            miss = jnp.concatenate([misses[2 * chunk], misses[2 * chunk + 1]], axis=1)
            ab = jnp.concatenate([hit / prob, miss / (1.0 - prob)], axis=0)
            a1, a2, a3 = split3(ab)
            x = nn(g96, a1)
            y = nn(g64, a2)
            sums = x[0:kdim] + (x[kdim : 2 * kdim] + y[0:kdim] + (x[2 * kdim :] + y[kdim:] + nn(g1, a3)))
            for half in range(2):
                for r in range(4):
                    part[e, r // 2, (r % 2) * blocks + 2 * chunk + half, 0:8, :] = sums[
                        8 * r : 8 * r + 8, 128 * half : 128 * half + 128
                    ]
            u = nt(a1, jnp.concatenate([q1, q2, q3], axis=0))
            w = nt(a2, jnp.concatenate([q1, q2], axis=0))
            cd += u[:, 0:kdim] + (
                u[:, kdim : 2 * kdim] + w[:, 0:kdim] + (u[:, 2 * kdim :] + w[:, kdim:] + nt(a3, q1))
            )
        fc = f * cd[0:128]
        f_next = fc / (fc + (1.0 - f) * cd[128:256])
        extra = extra_of(f_next)
        for c in range(2):
            for i in range(inds):
                part[e, c, i, 8:9, :] = extra
        pair = send(part.at[e, other], pair_in.at[e], pair_send.at[e], pair_recv.at[e], (me, other))
        pair.wait_recv()
        mine[e] = part[e, core] + pair_in[e]
        for j in peers:
            send(mine.at[e, j], scat_in.at[e, me], scat_send.at[e], scat_recv.at[e], (j, core))
        scat_in[e, me] = mine[e, me]
        arrived(scat_in.at[e, most], scat_recv.at[e])
        total = scat_in[e, 0]
        for i in range(1, inds):
            total = total + scat_in[e, i]
        full[e, core, me] = total[0:8]
        for j in peers:
            send(full.at[e, core, me], full.at[e, core, me], gath_send.at[e], gath_recv.at[e], (j, core))
        arrived(full.at[e, core, most], gath_recv.at[e])
        fwd = send(full.at[e, core], full.at[e, core], fwd_send.at[e], fwd_recv.at[e], (me, other))
        fwd.wait_recv()
        sums = jnp.concatenate(
            [
                jnp.concatenate([full[e, r // 2, (r % 2) * blocks + b] for b in range(blocks)], axis=1)
                for r in range(4)
            ],
            axis=0,
        )
        q_next = q_ref[...] * sums
        q_next = q_next / jnp.sum(q_next, axis=0, keepdims=True)
        pair.wait_send()
        fwd.wait_send()
        arrived(scat_in.at[e, most], scat_send.at[e])
        arrived(full.at[e, core, most], gath_send.at[e])
        return q_next, f_next, total[8:9]

    def one_step(step, carry):
        f0 = f_zero[...]
        q_first, f_first, _ = em_map(2 * step, q_zero, f0, lambda f: jnp.zeros((1, 128), f32))
        q_one[...] = q_first
        f_one[...] = f_first
        rf = f_first - f0
        rr_f = total_of(rf * rf)

        def lengths(f_next):
            vf = f_next - 2.0 * f_first + f0
            return jnp.where(lane == 0, rr_f, jnp.where(lane == 1, total_of(vf * vf), 0.0))

        q_two, f_two, row = em_map(2 * step + 1, q_one, f_one[...], lengths)
        q0 = q_zero[...]
        rq = q_one[...] - q0
        vq = q_two - 2.0 * q_one[...] + q0
        vf = f_two - 2.0 * f_first + f0
        first = total_of(rq * rq) + total_of(jnp.where(lane == 0, row, 0.0))
        second = total_of(vq * vq) + total_of(jnp.where(lane == 1, row, 0.0))
        alpha = -jnp.sqrt(first / (second + 1e-20))
        q_ext = jnp.clip(q0 - 2.0 * alpha * rq + alpha * alpha * vq, clip_low, 1.0 - clip_low)
        q_zero[...] = q_ext / jnp.sum(q_ext, axis=0, keepdims=True)
        f_zero[...] = jnp.clip(f0 - 2.0 * alpha * rf + alpha * alpha * vf, clip_low, 1.0 - clip_low)
        return carry

    lax.fori_loop(0, STEPS, one_step, 0)
    f_out[...] = f_zero[...]
    flip[...] = q_zero[:, pl.ds(pl.multiple_of(me // 2 * 128, 128), 128)].T
    q_out[...] = flip[pl.ds(pl.multiple_of(lax.rem(me, 2) * rows, rows), rows), :]


def fast_device(genotypes, observed, ancestry, freqs):
    inds = lax.axis_size("ind")
    rows, kdim = ancestry.shape
    people = rows * inds
    blocks = people // 128
    maps = 2 * STEPS
    dma = pltpu.SemaphoreType.DMA
    vmem = pl.BlockSpec(memory_space=pltpu.VMEM)
    return pl.pallas_call(
        functools.partial(kernel, inds),
        out_shape=(
            jax.ShapeDtypeStruct(ancestry.shape, f32),
            jax.ShapeDtypeStruct(freqs.shape, f32),
        ),
        in_specs=[vmem] * 4,
        out_specs=(vmem, vmem),
        scratch_shapes=[
            pltpu.VMEM((inds, rows, 128), jnp.int32),
            pltpu.VMEM((inds, rows, 128), jnp.int32),
            pltpu.VMEM((inds, rows, kdim), f32),
            pltpu.VMEM((blocks, 128, 128), f32),
            pltpu.VMEM((blocks, 128, 128), f32),
            pltpu.VMEM((maps, 2, inds, 9, 128), f32),
            pltpu.VMEM((maps, inds, 9, 128), f32),
            pltpu.VMEM((maps, inds, 9, 128), f32),
            pltpu.VMEM((maps, inds, 9, 128), f32),
            pltpu.VMEM((maps, 2, inds, 8, 128), f32),
            pltpu.VMEM((kdim, people), f32),
            pltpu.VMEM((kdim, people), f32),
            pltpu.VMEM((128, kdim), f32),
            pltpu.VMEM((128, kdim), f32),
            pltpu.VMEM((128, kdim), f32),
            dma, dma, dma, dma, dma, dma,
        ]
        + [dma((maps,))] * 8,
        compiler_params=pltpu.CompilerParams(
            collective_id=0, has_side_effects=True, vmem_limit_bytes=40 * 1024 * 1024
        ),
    )(genotypes, observed, ancestry, freqs)


def pick(genotypes, observed, ancestry, freqs):
    inds = lax.axis_size("ind")
    rows, kdim = ancestry.shape
    fits = (
        lax.axis_size("snp") == 2
        and freqs.shape[0] == 128
        and rows == 64
        and kdim == 32
        and inds % 4 == 0
        and (rows * inds // 128) * 2 == inds
    )
    form = fast_device if fits else per_device
    return form(genotypes, observed, ancestry, freqs)


def solution(mesh):
    in_specs = (P("ind", "snp"), P("ind", "snp"), P("ind", None), P(("snp", "ind"), None))
    out_specs = (P("ind", None), P(("snp", "ind"), None))
    return jax.shard_map(pick, mesh=mesh, in_specs=in_specs, out_specs=out_specs, check_vma=False)
```

profile of v0, /device:TPU:0, one launch (start us, length us, event | category | flops | bytes accessed | tf_op | source)
XLA Modules:
  0.0 127.6 jit_solution(3174742895006632510)
XLA Ops:
  0.6 0.0 copy-start.2
  0.6 0.8 copy.6.anc_ref
  1.4 0.0 copy-done.2
  1.4 0.1 copy.7.freq_ref
  1.5 0.0 copy-start
  1.6 1.0 copy-done
  2.6 0.0 copy-start.1
  2.6 1.0 copy-done.1
  3.6 122.6 %shard_map.59 = (f32[64,32]{1,0:T(8,128)S(1)}, f32[128,32]{1,0:T(8,128)S(1)}) custom-call(s32[64,2048]{1,0:T(8,128)S(1)} %copy-done, s32[64,2048]{1,0:T(8,128)S(1)} %copy-done.1, f32[64,32]{1,0:T(8,128)S(1)} %copy.6.anc_ref, f32[128,32]{1,0:T(8,128)S(1)} %copy.7.freq_ref), custom_call_target="tpu_custom_call" | custom-call | tf_op jit(solution)/shard_map/pallas_call | solution.py:256
  126.2 0.7 copy.8
  126.9 0.7 copy.9
Async XLA Ops:
  0.6 0.8 copy-start.2
  1.5 1.0 copy-start
  2.6 1.0 copy-start.1
where the time goes:
time: 128 us
  Pallas kernels  123 us (96%)
  local copies, waits for them, and re-layouts  4.34 us (3%)
    pallas_call x1, Pallas kernels, fast_device(): pl.pallas_call(functools.partial(kernel, inds), out_shape=(jax.ShapeDtype...  123 us
    unnamed x8, local copies, waits for them, and re-layouts  2.98 us

commit v1 on v0

v1 whole, which is shorter than its diff:
```python
import functools

import jax
import jax.numpy as jnp
from jax import lax
from jax.experimental import pallas as pl
from jax.experimental.pallas import tpu as pltpu
from jax.sharding import PartitionSpec as P

STEPS = 3


clip_low = 1e-05
high = lax.Precision.HIGHEST
MESH = pl.DeviceIdType.MESH
f32 = jnp.float32
bf16 = jnp.bfloat16


def over_rows(left, right):
    return lax.dot_general(
        left, right, (((0,), (0,)), ((), ())), precision=high, preferred_element_type=jnp.float32
    )


def per_device(genotypes, observed, ancestry, freqs):
    ind_count = lax.axis_size("ind")
    snp_count = lax.axis_size("snp")
    geno = genotypes.astype(jnp.float32)
    seen = observed.astype(jnp.float32)
    hits = seen * geno
    misses = seen * (2.0 - geno)
    own_rows = freqs.shape[0]
    q_zero = ancestry / jnp.sum(ancestry, axis=1, keepdims=True)
    f_zero = lax.all_gather(freqs, "ind", axis=0, tiled=True)
    f_weight = 1.0 / ind_count
    q_weight = 1.0 / snp_count

    def em_map(q_rows, f_state):
        prob = jnp.dot(q_rows, f_state.T, precision=high, preferred_element_type=jnp.float32)
        ratio_a = hits / prob
        ratio_b = misses / (1.0 - prob)
        sum_a = jnp.dot(ratio_a, f_state, precision=high, preferred_element_type=jnp.float32)
        sum_b = jnp.dot(ratio_b, 1.0 - f_state, precision=high, preferred_element_type=jnp.float32)
        c_part = over_rows(ratio_a, q_rows)
        d_part = over_rows(ratio_b, q_rows)
        sum_a, sum_b = lax.psum((sum_a, sum_b), "snp")
        q_next = q_rows * (sum_a + sum_b)
        q_next = q_next / jnp.sum(q_next, axis=1, keepdims=True)
        c_total, d_total = lax.psum((c_part, d_part), "ind")
        f_next = f_state * c_total / (f_state * c_total + (1.0 - f_state) * d_total)
        return (q_next, f_next)

    for step in range(STEPS):
        q_one, f_one = em_map(q_zero, f_zero)
        rq = q_one - q_zero
        rf = f_one - f_zero
        first_local = q_weight * jnp.sum(rq * rq) + f_weight * jnp.sum(rf * rf)
        q_two, f_two = em_map(q_one, f_one)
        vq = q_two - 2.0 * q_one + q_zero
        vf = f_two - 2.0 * f_one + f_zero
        second_local = q_weight * jnp.sum(vq * vq) + f_weight * jnp.sum(vf * vf)
        first, second = lax.psum((first_local, second_local), ("ind", "snp"))
        alpha = -jnp.sqrt(first / (second + 1e-20))
        q_ext = jnp.clip(q_zero - 2.0 * alpha * rq + alpha * alpha * vq, clip_low, 1.0 - clip_low)
        q_zero = q_ext / jnp.sum(q_ext, axis=1, keepdims=True)
        f_zero = jnp.clip(f_zero - 2.0 * alpha * rf + alpha * alpha * vf, clip_low, 1.0 - clip_low)
    f_final = lax.dynamic_slice_in_dim(f_zero, lax.axis_index("ind") * own_rows, own_rows, 0)
    return (q_zero, f_final)


def split3(x):
    one = x.astype(bf16)
    rest = x - one.astype(f32)
    two = rest.astype(bf16)
    three = (rest - two.astype(f32)).astype(bf16)
    return one, two, three


def nn(left, right):
    return jnp.dot(left, right, preferred_element_type=f32)


def nt(left, right):
    return lax.dot_general(left, right, (((1,), (1,)), ((), ())), preferred_element_type=f32)


def total_of(x):
    return jnp.sum(jnp.sum(x, axis=1, keepdims=True), axis=0, keepdims=True)


def kernel(
    inds, geno_ref, obs_ref, anc_ref, freq_ref, q_out, f_out,
    geno_all, obs_all, anc_all, hits, misses, part, pair_in, mine, scat_in, full,
    len_own, len_pair, len_sum, len_all,
    q_zero, q_one, f_zero, f_one, flip,
    anc_send, anc_recv, geno_send, obs_send, geno_recv, obs_recv,
    pair_send, pair_recv, scat_send, scat_recv, gath_send, gath_recv, fwd_send, fwd_recv,
    lp_send, lp_recv, la_send, la_recv,
):
    me = lax.axis_index("ind")
    core = lax.axis_index("snp")
    other = 1 - core
    rows = geno_ref.shape[0]
    chunks = hits.shape[0]
    blocks = 2 * chunks
    kdim = anc_ref.shape[1]
    width = inds.bit_length() - 1
    bits = [lax.rem(lax.div(me, 1 << k), 2) for k in range(width)]

    def flipped(d, low=0):
        j = 0
        for k in range(low, width):
            bit = 1 - bits[k] if (d >> k) & 1 else bits[k]
            j = j + bit * (1 << (k - low))
        return j

    peers = [(d, flipped(d)) for d in range(inds - 1, 0, -1)]

    barrier = pltpu.get_barrier_semaphore()
    for _, j in peers:
        pl.semaphore_signal(barrier, inc=1, device_id=(j, core), device_id_type=MESH)
    pl.semaphore_signal(barrier, inc=1, device_id=(me, other), device_id_type=MESH)
    pl.semaphore_wait(barrier, inds)

    def remote(src, dst, ssem, rsem, dev):
        return pltpu.make_async_remote_copy(
            src_ref=src, dst_ref=dst, send_sem=ssem, recv_sem=rsem,
            device_id=dev, device_id_type=MESH,
        )

    def send(*args):
        remote(*args).start()

    def arrived(ref, sem):
        pltpu.make_async_copy(ref, ref, sem).wait()

    most = pl.ds(0, inds - 1)
    for _, j in peers:
        send(anc_ref, anc_all.at[me], anc_send, anc_recv, (j, core))
    for d, j in peers:
        cols = pl.ds(pl.multiple_of(j * 128, 128), 128)
        send(geno_ref.at[:, cols], geno_all.at[me], geno_send, geno_recv.at[d // 4], (j, core))
        send(obs_ref.at[:, cols], obs_all.at[me], obs_send, obs_recv.at[d // 4], (j, core))
    own = pl.ds(pl.multiple_of(me * 128, 128), 128)
    geno_all[me] = geno_ref[:, own]
    obs_all[me] = obs_ref[:, own]
    anc_all[me] = anc_ref[...]
    f_zero[...] = freq_ref[...]
    arrived(anc_all.at[most], anc_recv)
    for chunk in range(chunks):
        anc = jnp.concatenate([anc_all[4 * chunk + s] for s in range(4)], axis=0).T
        q_zero[chunk] = anc / jnp.sum(anc, axis=0, keepdims=True)

    def lay(cc, chunk):
        count = pl.ds(0, 4 if cc else 3)
        arrived(geno_all.at[count], geno_recv.at[cc])
        arrived(obs_all.at[count], obs_recv.at[cc])
        for half in range(2):
            at = 4 * chunk + 2 * half
            geno = jnp.concatenate([geno_all[at], geno_all[at + 1]], axis=0).astype(f32).T
            seen = jnp.concatenate([obs_all[at], obs_all[at + 1]], axis=0).astype(f32).T
            hits[chunk, :, 128 * half : 128 * half + 128] = seen * geno
            misses[chunk, :, 128 * half : 128 * half + 128] = seen * (2.0 - geno)

    lane = lax.broadcasted_iota(jnp.int32, (8, 128), 1)

    def prepare(f):
        ft = f.T
        f1, f2, f3 = split3(ft)
        lhs = jnp.concatenate([x.astype(f32) for x in (f1, f2, f1, f2, f3, f1, f3, f2)], axis=0).T.astype(bf16)
        g1, g2, g3 = split3(jnp.concatenate([ft, 1.0 - ft], axis=1))
        return lhs, g1, jnp.concatenate([g1, g2], axis=0), jnp.concatenate([g1, g2, g3], axis=0)

    def em_map(e, q_ref, f, ready, is_first, lengths_of, step):
        lhs, g1, g64, g96 = ready
        kept = []
        for cc in range(chunks):
            chunk = flipped(4 * cc, 2) if is_first else cc
            if is_first:
                lay(cc, chunk)
            q1, q2, q3 = split3(q_ref[chunk])
            prob = nn(lhs, jnp.concatenate([q1, q1, q2, q2, q1, q3, q2, q3], axis=0))
            ab = jnp.concatenate([hits[chunk] / prob, misses[chunk] / (1.0 - prob)], axis=0)
            a1, a2, a3 = split3(ab)
            x = nn(g96, a1)
            y = nn(g64, a2)
            sums = x[0:kdim] + (x[kdim : 2 * kdim] + y[0:kdim] + (x[2 * kdim :] + y[kdim:] + nn(g1, a3)))
            for half in range(2):
                for r in range(4):
                    part[e, r // 2, (r % 2) * blocks + 2 * chunk + half] = sums[
                        8 * r : 8 * r + 8, 128 * half : 128 * half + 128
                    ]
            kept.append((a1, a2, a3, q1, q2, q3))

        pair = remote(part.at[e, other], pair_in.at[e], pair_send.at[e], pair_recv.at[e], (me, other))
        pair.start()

        def products(some):
            u = w = v = 0.0
            for a1, a2, a3, q1, q2, q3 in some:
                u = u + nt(a1, jnp.concatenate([q1, q2, q3], axis=0))
                w = w + nt(a2, jnp.concatenate([q1, q2], axis=0))
                v = v + nt(a3, q1)
            return u, w, v

        early = products(kept[: chunks // 2])
        pair.wait_recv()
        mine[e] = part[e, core] + pair_in[e]
        for _, j in peers:
            send(mine.at[e, j], scat_in.at[e, me], scat_send.at[e], scat_recv.at[e], (j, core))
        scat_in[e, me] = mine[e, me]
        late = products(kept[chunks // 2 :])
        u, w, v = [x + y for x, y in zip(early, late)]
        cd = u[:, 0:kdim] + (u[:, kdim : 2 * kdim] + w[:, 0:kdim] + (u[:, 2 * kdim :] + w[:, kdim:] + v))
        fc = f * cd[0:128]
        f_next = fc / (fc + (1.0 - f) * cd[128:256])
        if lengths_of is not None:
            len_own[step] = lengths_of(f_next)
            len_copy = remote(len_own.at[step], len_pair.at[step], lp_send.at[step], lp_recv.at[step], (me, other))
            len_copy.start()
        arrived(scat_in.at[e, most], scat_recv.at[e])
        total = scat_in[e, 0]
        for i in range(1, inds):
            total = total + scat_in[e, i]
        full[e, core, me] = total
        for d, j in peers:
            send(full.at[e, core, me], full.at[e, core, me], gath_send.at[e], gath_recv.at[e, d], (j, core))
        send(full.at[e, core, me], full.at[e, core, me], fwd_send.at[e], fwd_recv.at[e], (me, other))
        if lengths_of is not None:
            len_copy.wait_recv()
            len_sum[step] = len_own[step] + len_pair[step]
            for _, j in peers:
                send(len_sum.at[step], len_all.at[step, me], la_send.at[step], la_recv.at[step], (j, core))
            len_all[step, me] = len_sum[step]
            later = None
        else:
            later = prepare(f_next)
        for d, j in peers:
            slot = full.at[e, core, j]
            arrived(slot, gath_recv.at[e, d])
            send(slot, slot, fwd_send.at[e], fwd_recv.at[e], (me, other))
        lengths = None
        if lengths_of is not None:
            arrived(len_all.at[step, most], la_recv.at[step])
            lengths = len_all[step, 0]
            for i in range(1, inds):
                lengths = lengths + len_all[step, i]
            len_copy.wait_send()
            arrived(len_all.at[step, most], la_send.at[step])
        arrived(full.at[e, other], fwd_recv.at[e])
        q_next = []
        for chunk in range(chunks):
            sums = jnp.concatenate(
                [
                    jnp.concatenate(
                        [full[e, r // 2, (r % 2) * blocks + 2 * chunk + half] for half in range(2)], axis=1
                    )
                    for r in range(4)
                ],
                axis=0,
            )
            grown = q_ref[chunk] * sums
            q_next.append((grown / jnp.sum(grown, axis=0, keepdims=True))[None])
        pair.wait_send()
        arrived(scat_in.at[e, most], scat_send.at[e])
        arrived(full.at[e, core, most], gath_send.at[e])
        arrived(full.at[e, core], fwd_send.at[e])
        return jnp.concatenate(q_next, axis=0), f_next, later, lengths

    def all_sum(x):
        return total_of(jnp.sum(x, axis=0))

    def one_step(step, is_first):
        f0 = f_zero[...]
        q_first, f_first, ready, _ = em_map(2 * step, q_zero, f0, prepare(f0), is_first, None, step)
        q_one[...] = q_first
        f_one[...] = f_first

        def lengths_of(f_next):
            rf = f_first - f0
            vf = f_next - 2.0 * f_first + f0
            return jnp.where(lane == 0, total_of(rf * rf), jnp.where(lane == 1, total_of(vf * vf), 0.0))

        q_two, f_two, _, lengths = em_map(2 * step + 1, q_one, f_first, ready, False, lengths_of, step)
        q0 = q_zero[...]
        rq = q_one[...] - q0
        vq = q_two - 2.0 * q_one[...] + q0
        rf = f_first - f0
        vf = f_two - 2.0 * f_first + f0
        row = lengths[0:1]
        first = all_sum(rq * rq) + total_of(jnp.where(lane[0:1] == 0, row, 0.0))
        second = all_sum(vq * vq) + total_of(jnp.where(lane[0:1] == 1, row, 0.0))
        alpha = -jnp.sqrt(first / (second + 1e-20))
        q_ext = jnp.clip(q0 - 2.0 * alpha * rq + alpha * alpha * vq, clip_low, 1.0 - clip_low)
        q_zero[...] = q_ext / jnp.sum(q_ext, axis=1, keepdims=True)
        f_zero[...] = jnp.clip(f0 - 2.0 * alpha * rf + alpha * alpha * vf, clip_low, 1.0 - clip_low)

    one_step(0, True)
    arrived(anc_all.at[most], anc_send)
    arrived(geno_all.at[most], geno_send)
    arrived(obs_all.at[most], obs_send)

    def again(step, carry):
        one_step(step, False)
        return carry

    lax.fori_loop(1, STEPS, again, 0)
    f_out[...] = f_zero[...]
    flip[...] = q_zero[lax.div(me, 4)].T
    q_out[...] = flip[pl.ds(pl.multiple_of(lax.rem(me, 4) * rows, rows), rows), :]


def fast_device(genotypes, observed, ancestry, freqs):
    inds = lax.axis_size("ind")
    rows, kdim = ancestry.shape
    people = rows * inds
    chunks = people // 256
    maps = 2 * STEPS
    dma = pltpu.SemaphoreType.DMA
    vmem = pl.BlockSpec(memory_space=pltpu.VMEM)
    return pl.pallas_call(
        functools.partial(kernel, inds),
        out_shape=(
            jax.ShapeDtypeStruct(ancestry.shape, f32),
            jax.ShapeDtypeStruct(freqs.shape, f32),
        ),
        in_specs=[vmem] * 4,
        out_specs=(vmem, vmem),
        scratch_shapes=[
            pltpu.VMEM((inds, rows, 128), jnp.int32),
            pltpu.VMEM((inds, rows, 128), jnp.int32),
            pltpu.VMEM((inds, rows, kdim), f32),
            pltpu.VMEM((chunks, 128, 256), f32),
            pltpu.VMEM((chunks, 128, 256), f32),
            pltpu.VMEM((maps, 2, inds, 8, 128), f32),
            pltpu.VMEM((maps, inds, 8, 128), f32),
            pltpu.VMEM((maps, inds, 8, 128), f32),
            pltpu.VMEM((maps, inds, 8, 128), f32),
            pltpu.VMEM((maps, 2, inds, 8, 128), f32),
            pltpu.VMEM((STEPS, 8, 128), f32),
            pltpu.VMEM((STEPS, 8, 128), f32),
            pltpu.VMEM((STEPS, 8, 128), f32),
            pltpu.VMEM((STEPS, inds, 8, 128), f32),
            pltpu.VMEM((chunks, kdim, 256), f32),
            pltpu.VMEM((chunks, kdim, 256), f32),
            pltpu.VMEM((128, kdim), f32),
            pltpu.VMEM((128, kdim), f32),
            pltpu.VMEM((256, kdim), f32),
            dma, dma, dma, dma,
            dma((chunks,)),
            dma((chunks,)),
        ]
        + [dma((maps,))] * 5
        + [dma((maps, inds))]
        + [dma((maps,))] * 2
        + [dma((STEPS,))] * 4,
        compiler_params=pltpu.CompilerParams(
            collective_id=0, has_side_effects=True, vmem_limit_bytes=40 * 1024 * 1024
        ),
    )(genotypes, observed, ancestry, freqs)


def pick(genotypes, observed, ancestry, freqs):
    inds = lax.axis_size("ind")
    rows, kdim = ancestry.shape
    fits = (
        lax.axis_size("snp") == 2
        and freqs.shape[0] == 128
        and rows == 64
        and kdim == 32
        and inds >= 4
        and inds & (inds - 1) == 0
    )
    form = fast_device if fits else per_device
    return form(genotypes, observed, ancestry, freqs)


def solution(mesh):
    in_specs = (P("ind", "snp"), P("ind", "snp"), P("ind", None), P(("snp", "ind"), None))
    out_specs = (P("ind", None), P(("snp", "ind"), None))
    return jax.shard_map(pick, mesh=mesh, in_specs=in_specs, out_specs=out_specs, check_vma=False)
```

time: 128 us -> 125 us (0.977)
  Pallas kernels: 123 us -> 119 us
    pallas_call x1, Pallas kernels: 123 us -> 119 us  [fast_device(): pl.pallas_call(functools.partial(kernel, inds), out_shape=(jax.ShapeDtype...]
where the time goes in v1:
time: 125 us; the launch traced here: 124 us
  Pallas kernels  119 us (95%)
  local copies, waits for them, and re-layouts  4.34 us (3%)
    pallas_call x1, Pallas kernels, fast_device(): pl.pallas_call(functools.partial(kernel, inds), out_shape=(jax.ShapeDtype...  119 us
    unnamed x8, local copies, waits for them, and re-layouts  2.98 us

profile of v1, /device:TPU:0, one launch (start us, length us, event | category | flops | bytes accessed | tf_op | source)
XLA Modules:
  0.0 124.4 jit_solution(6000264045605658067)
XLA Ops:
  0.6 0.0 copy-start.2
  0.6 0.8 copy.6.anc_ref
  1.4 0.0 copy-done.2
  1.4 0.1 copy.7.freq_ref
  1.5 0.0 copy-start
  1.6 1.0 copy-done
  2.6 0.0 copy-start.1
  2.6 1.0 copy-done.1
  3.6 119.4 %shard_map.59 = (f32[64,32]{1,0:T(8,128)S(1)}, f32[128,32]{1,0:T(8,128)S(1)}) custom-call(s32[64,2048]{1,0:T(8,128)S(1)} %copy-done, s32[64,2048]{1,0:T(8,128)S(1)} %copy-done.1, f32[64,32]{1,0:T(8,128)S(1)} %copy.6.anc_ref, f32[128,32]{1,0:T(8,128)S(1)} %copy.7.freq_ref), custom_call_target="tpu_custom_call" | custom-call | tf_op jit(solution)/shard_map/pallas_call | solution.py:322
  123.0 0.7 copy.8
  123.7 0.7 copy.9
Async XLA Ops:
  0.6 0.8 copy-start.2
  1.5 1.0 copy-start
  2.6 1.0 copy-start.1

commit v2 on v1

--- a/solution.py
+++ b/solution.py
@@ -91,19 +91,18 @@
 
 def kernel(
     inds, geno_ref, obs_ref, anc_ref, freq_ref, q_out, f_out,
-    geno_all, obs_all, anc_all, hits, misses, part, pair_in, mine, scat_in, full,
-    len_own, len_pair, len_sum, len_all,
+    geno_all, obs_all, anc_all, hits, misses, part, rs_in, z_own, z_in, full,
+    len_own, len_in, len_sum, len_z,
     q_zero, q_one, f_zero, f_one, flip,
     anc_send, anc_recv, geno_send, obs_send, geno_recv, obs_recv,
-    pair_send, pair_recv, scat_send, scat_recv, gath_send, gath_recv, fwd_send, fwd_recv,
-    lp_send, lp_recv, la_send, la_recv,
+    rs_send, rs_recv, z_send, z_recv, ag_send, ag_recv,
+    lr_send, lr_recv, lz_send, lz_recv,
 ):
     me = lax.axis_index("ind")
     core = lax.axis_index("snp")
     other = 1 - core
     rows = geno_ref.shape[0]
     chunks = hits.shape[0]
-    blocks = 2 * chunks
     kdim = anc_ref.shape[1]
     width = inds.bit_length() - 1
     bits = [lax.rem(lax.div(me, 1 << k), 2) for k in range(width)]
@@ -117,11 +116,18 @@
 
     peers = [(d, flipped(d)) for d in range(inds - 1, 0, -1)]
 
+    group = core * 4 + lax.rem(me, 4)
+    layer = lax.div(me, 4)
+    near = [(flipped(d % 4), other if d >= 4 else core) for d in (7, 3, 6, 5, 2, 1, 4)]
+    near = [(j, c, c * 4 + lax.rem(j, 4)) for j, c in near]
+    columns = [(flipped(4 * d), core) for d in (3, 2, 1)]
+
     barrier = pltpu.get_barrier_semaphore()
     for _, j in peers:
         pl.semaphore_signal(barrier, inc=1, device_id=(j, core), device_id_type=MESH)
-    pl.semaphore_signal(barrier, inc=1, device_id=(me, other), device_id_type=MESH)
-    pl.semaphore_wait(barrier, inds)
+    for d in range(4):
+        pl.semaphore_signal(barrier, inc=1, device_id=(flipped(d), other), device_id_type=MESH)
+    pl.semaphore_wait(barrier, inds + 3)
 
     def remote(src, dst, ssem, rsem, dev):
         return pltpu.make_async_remote_copy(
@@ -150,7 +156,9 @@
     arrived(anc_all.at[most], anc_recv)
     for chunk in range(chunks):
         anc = jnp.concatenate([anc_all[4 * chunk + s] for s in range(4)], axis=0).T
-        q_zero[chunk] = anc / jnp.sum(anc, axis=0, keepdims=True)
+        anc = anc / jnp.sum(anc, axis=0, keepdims=True)
+        for half in range(2):
+            q_zero[2 * chunk + half] = anc[:, 128 * half : 128 * half + 128]
 
     def lay(cc, chunk):
         count = pl.ds(0, 4 if cc else 3)
@@ -172,6 +180,15 @@
         g1, g2, g3 = split3(jnp.concatenate([ft, 1.0 - ft], axis=1))
         return lhs, g1, jnp.concatenate([g1, g2], axis=0), jnp.concatenate([g1, g2, g3], axis=0)
 
+    seven = pl.ds(0, 7)
+    three = pl.ds(0, chunks - 1)
+
+    def added(ref, at, count):
+        total = ref[at, 0]
+        for i in range(1, count):
+            total = total + ref[at, i]
+        return total
+
     def em_map(e, q_ref, f, ready, is_first, lengths_of, step):
         lhs, g1, g64, g96 = ready
         kept = []
@@ -179,7 +196,7 @@
             chunk = flipped(4 * cc, 2) if is_first else cc
             if is_first:
                 lay(cc, chunk)
-            q1, q2, q3 = split3(q_ref[chunk])
+            q1, q2, q3 = split3(jnp.concatenate([q_ref[2 * chunk], q_ref[2 * chunk + 1]], axis=1))
             prob = nn(lhs, jnp.concatenate([q1, q1, q2, q2, q1, q3, q2, q3], axis=0))
             ab = jnp.concatenate([hits[chunk] / prob, misses[chunk] / (1.0 - prob)], axis=0)
             a1, a2, a3 = split3(ab)
@@ -187,14 +204,12 @@
             y = nn(g64, a2)
             sums = x[0:kdim] + (x[kdim : 2 * kdim] + y[0:kdim] + (x[2 * kdim :] + y[kdim:] + nn(g1, a3)))
             for half in range(2):
-                for r in range(4):
-                    part[e, r // 2, (r % 2) * blocks + 2 * chunk + half] = sums[
-                        8 * r : 8 * r + 8, 128 * half : 128 * half + 128
-                    ]
+                part[e, 2 * chunk + half] = sums[:, 128 * half : 128 * half + 128]
             kept.append((a1, a2, a3, q1, q2, q3))
 
-        pair = remote(part.at[e, other], pair_in.at[e], pair_send.at[e], pair_recv.at[e], (me, other))
-        pair.start()
+        for j, c, g in near:
+            send(part.at[e, g], rs_in.at[e, group], rs_send.at[e], rs_recv.at[e], (j, c))
+        rs_in[e, group] = part[e, group]
 
         def products(some):
             u = w = v = 0.0
@@ -205,11 +220,11 @@
             return u, w, v
 
         early = products(kept[: chunks // 2])
-        pair.wait_recv()
-        mine[e] = part[e, core] + pair_in[e]
-        for _, j in peers:
-            send(mine.at[e, j], scat_in.at[e, me], scat_send.at[e], scat_recv.at[e], (j, core))
-        scat_in[e, me] = mine[e, me]
+        arrived(rs_in.at[e, seven], rs_recv.at[e])
+        z_own[e] = added(rs_in, e, 8)
+        for dev in columns:
+            send(z_own.at[e], z_in.at[e, layer], z_send.at[e], z_recv.at[e], dev)
+        z_in[e, layer] = z_own[e]
         late = products(kept[chunks // 2 :])
         u, w, v = [x + y for x, y in zip(early, late)]
         cd = u[:, 0:kdim] + (u[:, kdim : 2 * kdim] + w[:, 0:kdim] + (u[:, 2 * kdim :] + w[:, kdim:] + v))
@@ -217,56 +232,33 @@
         f_next = fc / (fc + (1.0 - f) * cd[128:256])
         if lengths_of is not None:
             len_own[step] = lengths_of(f_next)
-            len_copy = remote(len_own.at[step], len_pair.at[step], lp_send.at[step], lp_recv.at[step], (me, other))
-            len_copy.start()
-        arrived(scat_in.at[e, most], scat_recv.at[e])
-        total = scat_in[e, 0]
-        for i in range(1, inds):
-            total = total + scat_in[e, i]
-        full[e, core, me] = total
-        for d, j in peers:
-            send(full.at[e, core, me], full.at[e, core, me], gath_send.at[e], gath_recv.at[e, d], (j, core))
-        send(full.at[e, core, me], full.at[e, core, me], fwd_send.at[e], fwd_recv.at[e], (me, other))
+            for j, c, g in near:
+                send(len_own.at[step], len_in.at[step, group], lr_send.at[step], lr_recv.at[step], (j, c))
+            len_in[step, group] = len_own[step]
+        arrived(z_in.at[e, three], z_recv.at[e])
+        grown = q_ref[group] * added(z_in, e, chunks)
+        full[e, group] = grown / jnp.sum(grown, axis=0, keepdims=True)
+        for j, c, g in near:
+            send(full.at[e, group], full.at[e, group], ag_send.at[e], ag_recv.at[e], (j, c))
+        later = lengths = None
         if lengths_of is not None:
-            len_copy.wait_recv()
-            len_sum[step] = len_own[step] + len_pair[step]
-            for _, j in peers:
-                send(len_sum.at[step], len_all.at[step, me], la_send.at[step], la_recv.at[step], (j, core))
-            len_all[step, me] = len_sum[step]
-            later = None
+            arrived(len_in.at[step, seven], lr_recv.at[step])
+            len_sum[step] = added(len_in, step, 8)
+            for dev in columns:
+                send(len_sum.at[step], len_z.at[step, layer], lz_send.at[step], lz_recv.at[step], dev)
+            len_z[step, layer] = len_sum[step]
         else:
             later = prepare(f_next)
-        for d, j in peers:
-            slot = full.at[e, core, j]
-            arrived(slot, gath_recv.at[e, d])
-            send(slot, slot, fwd_send.at[e], fwd_recv.at[e], (me, other))
-        lengths = None
+        arrived(full.at[e, seven], ag_recv.at[e])
         if lengths_of is not None:
-            arrived(len_all.at[step, most], la_recv.at[step])
-            lengths = len_all[step, 0]
-            for i in range(1, inds):
-                lengths = lengths + len_all[step, i]
-            len_copy.wait_send()
-            arrived(len_all.at[step, most], la_send.at[step])
-        arrived(full.at[e, other], fwd_recv.at[e])
-        q_next = []
-        for chunk in range(chunks):
-            sums = jnp.concatenate(
-                [
-                    jnp.concatenate(
-                        [full[e, r // 2, (r % 2) * blocks + 2 * chunk + half] for half in range(2)], axis=1
-                    )
-                    for r in range(4)
-                ],
-                axis=0,
-            )
-            grown = q_ref[chunk] * sums
-            q_next.append((grown / jnp.sum(grown, axis=0, keepdims=True))[None])
-        pair.wait_send()
-        arrived(scat_in.at[e, most], scat_send.at[e])
-        arrived(full.at[e, core, most], gath_send.at[e])
-        arrived(full.at[e, core], fwd_send.at[e])
-        return jnp.concatenate(q_next, axis=0), f_next, later, lengths
+            arrived(len_z.at[step, three], lz_recv.at[step])
+            lengths = added(len_z, step, chunks)
+            arrived(len_in.at[step, seven], lr_send.at[step])
+            arrived(len_z.at[step, three], lz_send.at[step])
+        arrived(rs_in.at[e, seven], rs_send.at[e])
+        arrived(z_in.at[e, three], z_send.at[e])
+        arrived(full.at[e, seven], ag_send.at[e])
+        return full[e], f_next, later, lengths
 
     def all_sum(x):
         return total_of(jnp.sum(x, axis=0))
@@ -307,8 +299,8 @@
 
     lax.fori_loop(1, STEPS, again, 0)
     f_out[...] = f_zero[...]
-    flip[...] = q_zero[lax.div(me, 4)].T
-    q_out[...] = flip[pl.ds(pl.multiple_of(lax.rem(me, 4) * rows, rows), rows), :]
+    flip[...] = q_zero[lax.div(me, 2)].T
+    q_out[...] = flip[pl.ds(pl.multiple_of(lax.rem(me, 2) * rows, rows), rows), :]
 
 
 def fast_device(genotypes, observed, ancestry, freqs):
@@ -333,27 +325,25 @@
             pltpu.VMEM((inds, rows, kdim), f32),
             pltpu.VMEM((chunks, 128, 256), f32),
             pltpu.VMEM((chunks, 128, 256), f32),
-            pltpu.VMEM((maps, 2, inds, 8, 128), f32),
-            pltpu.VMEM((maps, inds, 8, 128), f32),
-            pltpu.VMEM((maps, inds, 8, 128), f32),
-            pltpu.VMEM((maps, inds, 8, 128), f32),
-            pltpu.VMEM((maps, 2, inds, 8, 128), f32),
+            pltpu.VMEM((maps, 8, kdim, 128), f32),
+            pltpu.VMEM((maps, 8, kdim, 128), f32),
+            pltpu.VMEM((maps, kdim, 128), f32),
+            pltpu.VMEM((maps, chunks, kdim, 128), f32),
+            pltpu.VMEM((maps, 8, kdim, 128), f32),
             pltpu.VMEM((STEPS, 8, 128), f32),
+            pltpu.VMEM((STEPS, 8, 8, 128), f32),
             pltpu.VMEM((STEPS, 8, 128), f32),
-            pltpu.VMEM((STEPS, 8, 128), f32),
-            pltpu.VMEM((STEPS, inds, 8, 128), f32),
-            pltpu.VMEM((chunks, kdim, 256), f32),
-            pltpu.VMEM((chunks, kdim, 256), f32),
+            pltpu.VMEM((STEPS, chunks, 8, 128), f32),
+            pltpu.VMEM((8, kdim, 128), f32),
+            pltpu.VMEM((8, kdim, 128), f32),
             pltpu.VMEM((128, kdim), f32),
             pltpu.VMEM((128, kdim), f32),
-            pltpu.VMEM((256, kdim), f32),
+            pltpu.VMEM((128, kdim), f32),
             dma, dma, dma, dma,
             dma((chunks,)),
             dma((chunks,)),
         ]
-        + [dma((maps,))] * 5
-        + [dma((maps, inds))]
-        + [dma((maps,))] * 2
+        + [dma((maps,))] * 6
         + [dma((STEPS,))] * 4,
         compiler_params=pltpu.CompilerParams(
             collective_id=0, has_side_effects=True, vmem_limit_bytes=40 * 1024 * 1024
@@ -369,8 +359,7 @@
         and freqs.shape[0] == 128
         and rows == 64
         and kdim == 32
-        and inds >= 4
-        and inds & (inds - 1) == 0
+        and inds == 16
     )
     form = fast_device if fits else per_device
     return form(genotypes, observed, ancestry, freqs)

time: 125 us -> 121 us (0.968)
  Pallas kernels: 119 us -> 115 us
    pallas_call x1, Pallas kernels: 119 us -> 115 us  [fast_device(): pl.pallas_call(functools.partial(kernel, inds), out_shape=(jax.ShapeDtype...]
where the time goes in v2:
time: 121 us; the launch traced here: 120 us
  Pallas kernels  115 us (95%)
  local copies, waits for them, and re-layouts  4.34 us (4%)
    pallas_call x1, Pallas kernels, fast_device(): pl.pallas_call(functools.partial(kernel, inds), out_shape=(jax.ShapeDtype...  115 us
    unnamed x8, local copies, waits for them, and re-layouts  2.98 us

profile of v2, /device:TPU:0, one launch (start us, length us, event | category | flops | bytes accessed | tf_op | source)
XLA Modules:
  0.0 120.4 jit_solution(17147160206290823576)
XLA Ops:
  0.6 0.0 copy-start.2
  0.6 0.8 copy.6.anc_ref
  1.4 0.0 copy-done.2
  1.4 0.1 copy.7.freq_ref
  1.5 0.0 copy-start
  1.6 1.0 copy-done
  2.6 0.0 copy-start.1
  2.6 1.0 copy-done.1
  3.6 115.4 %shard_map.59 = (f32[64,32]{1,0:T(8,128)S(1)}, f32[128,32]{1,0:T(8,128)S(1)}) custom-call(s32[64,2048]{1,0:T(8,128)S(1)} %copy-done, s32[64,2048]{1,0:T(8,128)S(1)} %copy-done.1, f32[64,32]{1,0:T(8,128)S(1)} %copy.6.anc_ref, f32[128,32]{1,0:T(8,128)S(1)} %copy.7.freq_ref), custom_call_target="tpu_custom_call" | custom-call | tf_op jit(solution)/shard_map/pallas_call | solution.py:314
  119.0 0.7 copy.8
  119.7 0.7 copy.9
Async XLA Ops:
  0.6 0.8 copy-start.2
  1.5 1.0 copy-start
  2.6 1.0 copy-start.1

commit v3 on v2

--- a/solution.py
+++ b/solution.py
@@ -144,7 +144,8 @@
     most = pl.ds(0, inds - 1)
     for _, j in peers:
         send(anc_ref, anc_all.at[me], anc_send, anc_recv, (j, core))
-    for d, j in peers:
+    spread = [(4 * dz + d, flipped(4 * dz + d)) for d in (3, 1, 2, 0) for dz in (3, 2, 1, 0) if dz + d]
+    for d, j in spread:
         cols = pl.ds(pl.multiple_of(j * 128, 128), 128)
         send(geno_ref.at[:, cols], geno_all.at[me], geno_send, geno_recv.at[d // 4], (j, core))
         send(obs_ref.at[:, cols], obs_all.at[me], obs_send, obs_recv.at[d // 4], (j, core))
@@ -189,11 +190,18 @@
             total = total + ref[at, i]
         return total
 
+    def mixed(k):
+        low = lax.rem(lax.div(me, 2), 2)
+        return 2 * (other if k & 2 else core) + (1 - low if k & 1 else low)
+
+    def scatter(e, j, c, g):
+        send(part.at[e, g], rs_in.at[e, group], rs_send.at[e], rs_recv.at[e], (j, c))
+
     def em_map(e, q_ref, f, ready, is_first, lengths_of, step):
         lhs, g1, g64, g96 = ready
         kept = []
         for cc in range(chunks):
-            chunk = flipped(4 * cc, 2) if is_first else cc
+            chunk = flipped(4 * cc, 2) if is_first else mixed(3 - cc)
             if is_first:
                 lay(cc, chunk)
             q1, q2, q3 = split3(jnp.concatenate([q_ref[2 * chunk], q_ref[2 * chunk + 1]], axis=1))
@@ -206,9 +214,15 @@
             for half in range(2):
                 part[e, 2 * chunk + half] = sums[:, 128 * half : 128 * half + 128]
             kept.append((a1, a2, a3, q1, q2, q3))
-
-        for j, c, g in near:
-            send(part.at[e, g], rs_in.at[e, group], rs_send.at[e], rs_recv.at[e], (j, c))
+            if not is_first:
+                for half in range(2):
+                    g = 2 * chunk + half if cc < 3 else group + 1 - 2 * lax.rem(group, 2)
+                    if cc < 3 or half == 0:
+                        scatter(e, layer * 4 + lax.rem(g, 4), lax.div(g, 4), g)
+
+        if is_first:
+            for j, c, g in near:
+                scatter(e, j, c, g)
         rs_in[e, group] = part[e, group]
 
         def products(some):

time: 121 us -> 121 us (level)
  no operation moved by 1% of the time
where the time goes in v3:
time: 121 us
  Pallas kernels  116 us (96%)
  local copies, waits for them, and re-layouts  4.34 us (4%)
    pallas_call x1, Pallas kernels, fast_device(): pl.pallas_call(functools.partial(kernel, inds), out_shape=(jax.ShapeDtype...  116 us
    unnamed x8, local copies, waits for them, and re-layouts  2.98 us

profile of v3, /device:TPU:0, one launch (start us, length us, event | category | flops | bytes accessed | tf_op | source)
XLA Modules:
  0.0 121.0 jit_solution(4630360138713909201)
XLA Ops:
  0.6 0.0 copy-start.2
  0.6 0.8 copy.6.anc_ref
  1.4 0.0 copy-done.2
  1.4 0.1 copy.7.freq_ref
  1.5 0.0 copy-start
  1.6 1.0 copy-done
  2.6 0.0 copy-start.1
  2.6 1.0 copy-done.1
  3.6 116.0 %shard_map.59 = (f32[64,32]{1,0:T(8,128)S(1)}, f32[128,32]{1,0:T(8,128)S(1)}) custom-call(s32[64,2048]{1,0:T(8,128)S(1)} %copy-done, s32[64,2048]{1,0:T(8,128)S(1)} %copy-done.1, f32[64,32]{1,0:T(8,128)S(1)} %copy.6.anc_ref, f32[128,32]{1,0:T(8,128)S(1)} %copy.7.freq_ref), custom_call_target="tpu_custom_call" | custom-call | tf_op jit(solution)/shard_map/pallas_call | solution.py:328
  119.6 0.7 copy.8
  120.3 0.7 copy.9
Async XLA Ops:
  0.6 0.8 copy-start.2
  1.5 1.0 copy-start
  2.6 1.0 copy-start.1

commit v4 on v2

--- a/solution.py
+++ b/solution.py
@@ -96,7 +96,7 @@
     q_zero, q_one, f_zero, f_one, flip,
     anc_send, anc_recv, geno_send, obs_send, geno_recv, obs_recv,
     rs_send, rs_recv, z_send, z_recv, ag_send, ag_recv,
-    lr_send, lr_recv, lz_send, lz_recv,
+    lr_send, lr_recv, lz_send, lz_recv, own_sem,
 ):
     me = lax.axis_index("ind")
     core = lax.axis_index("snp")
@@ -149,10 +149,14 @@
         send(geno_ref.at[:, cols], geno_all.at[me], geno_send, geno_recv.at[d // 4], (j, core))
         send(obs_ref.at[:, cols], obs_all.at[me], obs_send, obs_recv.at[d // 4], (j, core))
     own = pl.ds(pl.multiple_of(me * 128, 128), 128)
-    geno_all[me] = geno_ref[:, own]
-    obs_all[me] = obs_ref[:, own]
+    geno_own = pltpu.make_async_copy(geno_ref.at[:, own], geno_all.at[me], own_sem.at[0])
+    obs_own = pltpu.make_async_copy(obs_ref.at[:, own], obs_all.at[me], own_sem.at[1])
+    geno_own.start()
+    obs_own.start()
     anc_all[me] = anc_ref[...]
     f_zero[...] = freq_ref[...]
+    geno_own.wait()
+    obs_own.wait()
     arrived(anc_all.at[most], anc_recv)
     for chunk in range(chunks):
         anc = jnp.concatenate([anc_all[4 * chunk + s] for s in range(4)], axis=0).T
@@ -317,7 +321,7 @@
             jax.ShapeDtypeStruct(ancestry.shape, f32),
             jax.ShapeDtypeStruct(freqs.shape, f32),
         ),
-        in_specs=[vmem] * 4,
+        in_specs=[pl.BlockSpec(memory_space=pl.ANY)] * 2 + [vmem] * 2,
         out_specs=(vmem, vmem),
         scratch_shapes=[
             pltpu.VMEM((inds, rows, 128), jnp.int32),
@@ -344,7 +348,8 @@
             dma((chunks,)),
         ]
         + [dma((maps,))] * 6
-        + [dma((STEPS,))] * 4,
+        + [dma((STEPS,))] * 4
+        + [dma((2,))],
         compiler_params=pltpu.CompilerParams(
             collective_id=0, has_side_effects=True, vmem_limit_bytes=40 * 1024 * 1024
         ),

time: 121 us -> 121 us (level)
  no operation moved by 1% of the time
where the time goes in v4:
time: 121 us; the launch traced here: 120 us
  Pallas kernels  115 us (95%)
  local copies, waits for them, and re-layouts  4.34 us (4%)
    pallas_call x1, Pallas kernels, fast_device(): pl.pallas_call(functools.partial(kernel, inds), out_shape=(jax.ShapeDtype...  115 us
    unnamed x8, local copies, waits for them, and re-layouts  2.98 us

profile of v4, /device:TPU:0, one launch (start us, length us, event | category | flops | bytes accessed | tf_op | source)
XLA Modules:
  0.0 120.4 jit_solution(10380547722435873803)
XLA Ops:
  0.6 0.0 copy-start.2
  0.6 0.8 copy.6.anc_ref
  1.4 0.0 copy-done.2
  1.4 0.1 copy.7.freq_ref
  1.5 0.0 copy-start
  1.6 1.0 copy-done
  2.6 0.0 copy-start.1
  2.6 1.0 copy-done.1
  3.6 115.4 %shard_map.59 = (f32[64,32]{1,0:T(8,128)S(1)}, f32[128,32]{1,0:T(8,128)S(1)}) custom-call(s32[64,2048]{1,0:T(8,128)S(1)} %copy-done, s32[64,2048]{1,0:T(8,128)S(1)} %copy-done.1, f32[64,32]{1,0:T(8,128)S(1)} %copy.6.anc_ref, f32[128,32]{1,0:T(8,128)S(1)} %copy.7.freq_ref), custom_call_target="tpu_custom_call" | custom-call | tf_op jit(solution)/shard_map/pallas_call | solution.py:318
  119.0 0.7 copy.8
  119.7 0.7 copy.9
Async XLA Ops:
  0.6 0.8 copy-start.2
  1.5 1.0 copy-start
  2.6 1.0 copy-start.1

commit v5 on v4

--- a/solution.py
+++ b/solution.py
@@ -202,7 +202,9 @@
                 lay(cc, chunk)
             q1, q2, q3 = split3(jnp.concatenate([q_ref[2 * chunk], q_ref[2 * chunk + 1]], axis=1))
             prob = nn(lhs, jnp.concatenate([q1, q1, q2, q2, q1, q3, q2, q3], axis=0))
-            ab = jnp.concatenate([hits[chunk] / prob, misses[chunk] / (1.0 - prob)], axis=0)
+            rest = 1.0 - prob
+            inverse = 1.0 / (prob * rest)
+            ab = jnp.concatenate([hits[chunk] * (rest * inverse), misses[chunk] * (prob * inverse)], axis=0)
             a1, a2, a3 = split3(ab)
             x = nn(g96, a1)
             y = nn(g64, a2)

time: 121 us -> 121 us (level)
  no operation moved by 1% of the time
where the time goes in v5:
time: 121 us
  Pallas kernels  116 us (96%)
  local copies, waits for them, and re-layouts  4.34 us (4%)
    pallas_call x1, Pallas kernels, fast_device(): pl.pallas_call(functools.partial(kernel, inds), out_shape=(jax.ShapeDtype...  116 us
    unnamed x8, local copies, waits for them, and re-layouts  2.98 us

profile of v5, /device:TPU:0, one launch (start us, length us, event | category | flops | bytes accessed | tf_op | source)
XLA Modules:
  0.0 120.6 jit_solution(5761615190332675801)
XLA Ops:
  0.6 0.0 copy-start.2
  0.6 0.8 copy.6.anc_ref
  1.4 0.0 copy-done.2
  1.4 0.1 copy.7.freq_ref
  1.5 0.0 copy-start
  1.6 1.0 copy-done
  2.6 0.0 copy-start.1
  2.6 1.0 copy-done.1
  3.6 115.6 %shard_map.59 = (f32[64,32]{1,0:T(8,128)S(1)}, f32[128,32]{1,0:T(8,128)S(1)}) custom-call(s32[64,2048]{1,0:T(8,128)S(1)} %copy-done, s32[64,2048]{1,0:T(8,128)S(1)} %copy-done.1, f32[64,32]{1,0:T(8,128)S(1)} %copy.6.anc_ref, f32[128,32]{1,0:T(8,128)S(1)} %copy.7.freq_ref), custom_call_target="tpu_custom_call" | custom-call | tf_op jit(solution)/shard_map/pallas_call | solution.py:320
  119.2 0.7 copy.8
  119.9 0.7 copy.9
Async XLA Ops:
  0.6 0.8 copy-start.2
  1.5 1.0 copy-start
  2.6 1.0 copy-start.1
